TPU v7x, 32 devices: a whole 2x2x4 slice. The times are simulated.
32 devices in a mesh: grp: 2 (over y), mesh: 16 (over z, x, core).
Axes of the slice: x: 2, y: 2, z: 4, core: 2. Of those that a mesh axis runs over, the one named last changes fastest.
Arguments:
- basis: bfloat16 [65536, 512], P(('grp', 'mesh')), parts along dimension 0, may hold values from -6 to 6
- blocks: bfloat16 [2, 512, 3, 128, 128], P(None, ('grp', 'mesh')), parts along dimension 1, may hold values from -0.0017089844 to 0.0017089844
- columns: int32 [2, 512, 2], P(None, ('grp', 'mesh')), parts along dimension 1, may hold values from 0 to 31
- sends: int32 [32, 16], P(('grp', 'mesh')), parts along dimension 0, may hold values from 0 to 15
Outputs:
- projected: float32 [1024, 1024], P(('grp', 'mesh')), parts along dimension 0
There are 2 independent parts, one for each index of `grp`. A program takes and returns all parts, laid end to end along the dimension named above; each array names one. Nothing has to cross between parts.
All inputs are finite; a program needn't handle non-finite values.
Results may differ from a plain program's by a relative error of at most 0.0029.
Values may be sent and summed in bfloat16 or wider, within the bound.
No kernel may reach another device: no remote copies, remote signals or barrier semaphores. Data moves between devices by JAX's collectives and lax.ppermute only.
A program may use at most 64 MiB of HBM per device.

v0:
```python
import jax
import jax.numpy as jnp
from jax import lax
from jax.experimental import pallas as pl
from jax.experimental.pallas import tpu as pltpu
from jax.sharding import PartitionSpec as P

AXIS = "mesh"
VMEM_BYTES = 28 * 1024 * 1024


def pairs(count, first):
    both = []
    for low in range(first, count - 1, 2):
        both += [(low, low + 1), (low + 1, low)]
    return both


def pick_blocks(own, sends, far):
    halo = sends.shape[1] // 2

    def kernel(sends_ref, own_ref, out_ref, sems):
        odd = lax.rem(lax.axis_index(AXIS), 2)
        first = (odd if far else 1 - odd) * halo
        copies = []
        for place in range(halo):
            block = sends_ref[0, first + place]
            copies.append(
                pltpu.make_async_copy(own_ref.at[block], out_ref.at[place], sems.at[place])
            )
        for copy in copies:
            copy.start()
        for copy in copies:
            copy.wait()

    size = halo * own.shape[1] * own.shape[2] * own.dtype.itemsize
    return pl.pallas_call(
        kernel,
        out_shape=jax.ShapeDtypeStruct((halo,) + own.shape[1:], own.dtype),
        in_specs=[pl.BlockSpec(memory_space=pltpu.SMEM), pl.BlockSpec(memory_space=pl.ANY)],
        out_specs=pl.BlockSpec(memory_space=pltpu.VMEM),
        scratch_shapes=[pltpu.SemaphoreType.DMA((halo,))],
        compiler_params=pltpu.CompilerParams(vmem_limit_bytes=VMEM_BYTES),
        cost_estimate=pl.CostEstimate(flops=0, bytes_accessed=2 * size, transcendentals=0),
    )(sends, own)


def own_terms(own, blocks, columns):
    params, count, slots, size, _ = blocks.shape
    width = own.shape[2]

    def kernel(columns_ref, own_ref, blocks_ref, out_ref):
        @pl.loop(0, count, unroll=2)
        def _(row):
            at = pl.ds(pl.multiple_of(row * size, size), size)
            for param in range(params):
                left, right = [blocks_ref[param, row, 0]], [own_ref[row]]
                for slot in range(1, slots):
                    block = blocks_ref[param, row, slot]
                    column = columns_ref[param, row, slot - 1]
                    left.append(jnp.where(column < count, block, jnp.zeros_like(block)))
                    right.append(own_ref[jnp.minimum(column, count - 1)])
                out_ref[param, at] = jnp.dot(
                    jnp.concatenate(left, axis=1),
                    jnp.concatenate(right, axis=0),
                    preferred_element_type=jnp.float32,
                )

    vmem = pl.BlockSpec(memory_space=pltpu.VMEM)
    terms = jax.ShapeDtypeStruct((params, count * size, width), jnp.float32)
    return pl.pallas_call(
        kernel,
        out_shape=terms,
        in_specs=[pl.BlockSpec(memory_space=pltpu.SMEM), vmem, vmem],
        out_specs=vmem,
        compiler_params=pltpu.CompilerParams(vmem_limit_bytes=VMEM_BYTES),
        cost_estimate=pl.CostEstimate(
            flops=2 * slots * size * terms.size,
            bytes_accessed=4 * terms.size + 2 * (own.size + blocks.size),
            transcendentals=0,
        ),
    )(columns, own, blocks)


def project(turned, terms, far, near, blocks, columns):
    params, count, slots, size, _ = blocks.shape
    halo, _, width = far.shape
    half = turned.shape[0] // 2

    def kernel(
        columns_ref, turned_ref, terms_ref, far_ref, near_ref, blocks_ref,
        keep_ref, give_ref, list_ref, image_ref,
    ):
        odd = lax.rem(lax.axis_index(AXIS), 2)
        list_ref[pl.ds(odd * halo, halo)] = far_ref[...]
        list_ref[pl.ds((1 - odd) * halo, halo)] = near_ref[...]

        @pl.loop(0, count, unroll=2)
        def _(row):
            at = pl.ds(pl.multiple_of(row * size, size), size)
            for param in range(params):
                left, right = [], []
                for slot in range(1, slots):
                    block = blocks_ref[param, row, slot]
                    column = columns_ref[param, row, slot - 1]
                    left.append(jnp.where(column < count, jnp.zeros_like(block), block))
                    right.append(list_ref[jnp.maximum(column - count, 0)])
                image = terms_ref[param, at] + jnp.dot(
                    jnp.concatenate(left, axis=1),
                    jnp.concatenate(right, axis=0),
                    preferred_element_type=jnp.float32,
                )
                image_ref[at, pl.ds(param * width, width)] = image.astype(image_ref.dtype)

        mine = pl.ds(pl.multiple_of(odd * half, half), half)
        other = pl.ds(pl.multiple_of((1 - odd) * half, half), half)
        step = 256 if width % 256 == 0 else width
        for at in range(0, params * width, step):
            cols = pl.ds(at, step)
            give_ref[:, cols] = jnp.dot(
                turned_ref[other], image_ref[:, cols], preferred_element_type=jnp.float32
            ).astype(give_ref.dtype)
            keep_ref[:, cols] = jnp.dot(
                turned_ref[mine], image_ref[:, cols], preferred_element_type=jnp.float32
            )

    vmem = pl.BlockSpec(memory_space=pltpu.VMEM)
    flops = 2 * params * count * size * width * ((slots - 1) * size + 2 * half)
    moved = 4 * terms.size + 2 * (turned.size + 2 * far.size + blocks.size)
    return pl.pallas_call(
        kernel,
        out_shape=(
            jax.ShapeDtypeStruct((half, params * width), jnp.float32),
            jax.ShapeDtypeStruct((half, params * width), jnp.bfloat16),
        ),
        in_specs=[pl.BlockSpec(memory_space=pltpu.SMEM)] + [vmem] * 5,
        out_specs=(vmem,) * 2,
        scratch_shapes=[
            pltpu.VMEM((2 * halo, size, width), far.dtype),
            pltpu.VMEM((count * size, params * width), jnp.bfloat16),
        ],
        compiler_params=pltpu.CompilerParams(vmem_limit_bytes=VMEM_BYTES),
        cost_estimate=pl.CostEstimate(flops=flops, bytes_accessed=moved, transcendentals=0),
    )(columns, turned, terms, far, near, blocks)


def shards(basis, blocks, columns, sends):
    params, count, _, size, _ = blocks.shape
    width = basis.shape[1]
    devices = lax.axis_size(AXIS)
    chips = devices // 2
    rows = width // devices
    own = basis.reshape(count, size, width)

    far = pick_blocks(own, sends, True)
    from_far = lax.ppermute(far, AXIS, pairs(devices, 1))
    near = pick_blocks(own, sends, False)
    from_near = lax.ppermute(near, AXIS, pairs(devices, 0))
    turned = basis.T.reshape(chips, 2, rows, count * size)
    turned = turned.transpose(1, 0, 2, 3).reshape(width, count * size)

    terms = own_terms(own, blocks, columns)

    keep, give = project(turned, terms, from_far, from_near, blocks, columns)
    taken = lax.ppermute(give, AXIS, pairs(devices, 0))
    chip_sum = (keep + taken.astype(jnp.float32)).astype(jnp.bfloat16)
    groups = [list(range(core, devices, 2)) for core in range(2)]
    parts = lax.all_to_all(
        chip_sum.reshape(chips, rows, params * width), AXIS,
        split_axis=0, concat_axis=0, axis_index_groups=groups, tiled=True,
    )
    return jnp.sum(parts.astype(jnp.float32), axis=0)


def solution(mesh):
    placed = (
        P(("grp", "mesh"), None),
        P(None, ("grp", "mesh"), None, None, None),
        P(None, ("grp", "mesh"), None),
        P(("grp", "mesh"), None),
    )
    return jax.shard_map(
        shards, mesh=mesh, in_specs=placed, out_specs=P(("grp", "mesh"), None), check_vma=False
    )
```

profile of v0, /device:TPU:0, one launch (start us, length us, event | category | flops | bytes accessed | tf_op | source)
XLA Modules:
  0.0 62.9 jit_solution(13451216468010473103)
XLA Ops:
  0.0 0.0 copy-start
  0.0 1.6 %copy-done = bf16[2048,512]{1,0:T(8,128)(2,1)S(1)} copy-done((bf16[2048,512]{1,0:T(8,128)(2,1)S(1)}, bf16[2048,512]{1,0:T(8,128)(2,1)}, u32[]{:S(2)}) %copy-start) | copy-done | bytes 2097176
  1.6 0.0 copy-start.3
  1.6 0.7 %copy-done.3 = s32[1,16]{1,0:T(1,128)S(1)} copy-done((s32[1,16]{1,0:T(1,128)S(1)}, s32[1,16]{1,0:T(1,128)}, u32[]{:S(2)}) %copy-start.3) | copy-done | bytes 88
  2.2 3.0 %shard_map.47 = bf16[8,128,512]{2,1,0:T(8,128)(2,1)} custom-call(s32[1,16]{1,0:T(1,128)S(1)} %copy-done.3, bf16[16,128,512]{2,1,0:T(8,128)(2,1)S(1)} %bitcast.8), custom_call_target="tpu_custom_call" | custom-call | bytes 2097152 | tf_op jit(solution)/shard_map/pallas_call | solution.py:37
  5.2 0.0 copy-start.1
  5.3 0.9 %collective-permute-start = (bf16[8,128,512]{2,1,0:T(8,128)(2,1)}, bf16[8,128,512]{2,1,0:T(8,128)(2,1)S(1)}, u32[]{:S(2)}, u32[]{:S(2)}) collective-permute-start(bf16[8,128,512]{2,1,0:T(8,128)(2,1)} %shard_map.47), channel_id=1, source_target_pairs={{1,2},{2,1},{3,4},{4,3},{5,6},{6,5},{7,8},{8,7},{9,10},{10,9},{11,... | collective-permute-start | bytes 3145736 | tf_op jit(solution)/shard_map/ppermute | solution.py:156
  6.1 3.0 %shard_map.48 = bf16[8,128,512]{2,1,0:T(8,128)(2,1)} custom-call(s32[1,16]{1,0:T(1,128)S(1)} %copy-done.3, bf16[16,128,512]{2,1,0:T(8,128)(2,1)S(1)} %bitcast.9), custom_call_target="tpu_custom_call" | custom-call | bytes 2097152 | tf_op jit(solution)/shard_map/pallas_call | solution.py:37
  9.1 0.0 copy-start.4
  9.1 4.3 %collective-permute-start.1 = (bf16[8,128,512]{2,1,0:T(8,128)(2,1)}, bf16[8,128,512]{2,1,0:T(8,128)(2,1)}, u32[]{:S(2)}, u32[]{:S(2)}) collective-permute-start(bf16[8,128,512]{2,1,0:T(8,128)(2,1)} %shard_map.48), channel_id=1, source_target_pairs={{0,1},{1,0},{2,3},{3,2},{4,5},{5,4},{6,7},{7,6},{8,9},{9,8},{10,11... | collective-permute-start | bytes 3145736 | tf_op jit(solution)/shard_map/ppermute | solution.py:158
  13.4 0.0 copy-done.1
  13.4 2.4 %copy.8 = bf16[2048,512]{0,1:T(8,128)(2,1)} copy(bf16[2048,512]{1,0:T(8,128)(2,1)S(1)} %copy-done.1) | data formatting | bytes 4194304 | tf_op args[0]
  15.9 0.0 copy-done.4
  15.9 0.1 copy.11.columns_ref
  16.0 0.0 copy-start.2
  16.0 2.0 %copy.9 = bf16[2,8,32,2048]{3,2,1,0:T(8,128)(2,1)S(1)} copy(bf16[2,8,32,2048]{3,2,0,1:T(8,128)(2,1)} %bitcast.12) | data formatting | bytes 4194304 | tf_op jit(solution)/shard_map/transpose | solution.py:160
  17.9 0.5 copy-done.2
  18.5 4.3 %shard_map.46.terms_ref = f32[2,2048,512]{2,1,0:T(8,128)S(1)} custom-call(s32[2,16,2]{2,1,0:T(8,128)S(1)} %copy.11.columns_ref, bf16[16,128,512]{2,1,0:T(8,128)(2,1)S(1)} %bitcast.10, bf16[2,16,3,128,128]{4,3,2,1,0:T(8,128)(2,1)S(1)} %copy-done.2), custom_call_target="tpu_custom_call" | custom-call | flops 1610612736 | bytes 13631488 | tf_op jit(solution)/shard_map/pallas_call | solution.py:71
  22.8 0.0 collective-permute-done.far_ref
  22.8 0.0 collective-permute-done.1.near_ref
  22.9 6.2 %shard_map.49 = (f32[256,1024]{1,0:T(8,128)S(1)}, bf16[256,1024]{1,0:T(8,128)(2,1)S(1)}) custom-call(s32[2,16,2]{2,1,0:T(8,128)S(1)} %copy.11.columns_ref, bf16[512,2048]{1,0:T(8,128)(2,1)S(1)} %bitcast.11, f32[2,2048,512]{2,1,0:T(8,128)S(1)} %shard_map.46.terms_ref, bf16[8,128,512]{2,1,0:T(8,128)(2,1)S(1)} %collective-permute-done.far_ref, ...), custom_call_target="tpu_custom_call" | custom-call | flops 3221225472 | bytes 15728640 | tf_op jit(solution)/shard_map/pallas_call | solution.py:130
  29.1 10.9 %collective-permute-start.2 = (bf16[256,1024]{1,0:T(8,128)(2,1)S(1)}, bf16[256,1024]{1,0:T(8,128)(2,1)S(1)}, u32[]{:S(2)}, u32[]{:S(2)}) collective-permute-start(bf16[256,1024]{1,0:T(8,128)(2,1)S(1)} %get-tuple-element.8), channel_id=1, source_target_pairs={{0,1},{1,0},{2,3},{3,2},{4,5},{5,4},{6,7},{7,6},{8,9},{9,8},{10,11... | collective-permute-start | bytes 1572872 | tf_op jit(solution)/shard_map/ppermute | solution.py:165
  40.0 1.5 %collective-permute-done.2 = bf16[256,1024]{1,0:T(8,128)(2,1)S(1)} collective-permute-done((bf16[256,1024]{1,0:T(8,128)(2,1)S(1)}, bf16[256,1024]{1,0:T(8,128)(2,1)S(1)}, u32[]{:S(2)}, u32[]{:S(2)}) %collective-permute-start.2) | collective-permute-done | bytes 524320 | tf_op jit(solution)/shard_map/ppermute | solution.py:165
  41.5 0.1 add_convert_fusion
  41.7 20.5 %all_to_all.5 = bf16[8,32,1024]{2,1,0:T(8,128)(2,1)S(1)} all-to-all(bf16[8,32,1024]{2,1,0:T(8,128)(2,1)S(1)} %bitcast.13), channel_id=1, replica_groups={{0,2,4,6,8,10,12,14},{1,3,5,7,9,11,13,15},{16,18,20,22,24,26,28,30},{17..., dimensions={0} | all-to-all | bytes 1048576 | tf_op jit(solution)/shard_map/all_to_all | solution.py:168
  62.2 0.7 %convert_reduce_fusion = f32[32,1024]{1,0:T(8,128)} fusion(bf16[8,32,1024]{2,1,0:T(8,128)(2,1)S(1)} %all_to_all.5), kind=kLoop, calls=%fused_computation | loop fusion | flops 491520 | bytes 655360 | tf_op jit(solution)/shard_map/reduce_sum | solution.py:172
Async XLA Ops:
  0.0 1.6 %copy-start = (bf16[2048,512]{1,0:T(8,128)(2,1)S(1)}, bf16[2048,512]{1,0:T(8,128)(2,1)}, u32[]{:S(2)}) copy-start(bf16[2048,512]{1,0:T(8,128)(2,1)} %param.4) | copy-start | bytes 6291460
  1.6 0.7 %copy-start.3 = (s32[1,16]{1,0:T(1,128)S(1)}, s32[1,16]{1,0:T(1,128)}, u32[]{:S(2)}) copy-start(s32[1,16]{1,0:T(1,128)} %sends_ref.3) | copy-start | bytes 196
  5.2 8.2 %copy-start.1 = (bf16[2048,512]{1,0:T(8,128)(2,1)S(1)}, bf16[2048,512]{1,0:T(8,128)(2,1)}, u32[]{:S(2)}) copy-start(bf16[2048,512]{1,0:T(8,128)(2,1)} %param.4) | copy-start | bytes 6291460
  5.3 17.6 %collective-permute-start = (bf16[8,128,512]{2,1,0:T(8,128)(2,1)}, bf16[8,128,512]{2,1,0:T(8,128)(2,1)S(1)}, u32[]{:S(2)}, u32[]{:S(2)}) collective-permute-start(bf16[8,128,512]{2,1,0:T(8,128)(2,1)} %shard_map.47), channel_id=1, source_target_pairs={{1,2},{2,1},{3,4},{4,3},{5,6},{6,5},{7,8},{8,7},{9,10},{10,9},{11,... | collective-permute-start | bytes 3145736 | tf_op jit(solution)/shard_map/ppermute | solution.py:156
  9.1 6.8 %copy-start.4 = (s32[2,16,2]{1,2,0:T(2,128)S(1)}, s32[2,16,2]{1,2,0:T(2,128)}, u32[]{:S(2)}) copy-start(s32[2,16,2]{1,2,0:T(2,128)} %param.6) | copy-start | bytes 772
  9.1 13.7 %collective-permute-start.1 = (bf16[8,128,512]{2,1,0:T(8,128)(2,1)}, bf16[8,128,512]{2,1,0:T(8,128)(2,1)}, u32[]{:S(2)}, u32[]{:S(2)}) collective-permute-start(bf16[8,128,512]{2,1,0:T(8,128)(2,1)} %shard_map.48), channel_id=1, source_target_pairs={{0,1},{1,0},{2,3},{3,2},{4,5},{5,4},{6,7},{7,6},{8,9},{9,8},{10,11... | collective-permute-start | bytes 3145736 | tf_op jit(solution)/shard_map/ppermute | solution.py:158
  16.0 2.5 %copy-start.2 = (bf16[2,16,3,128,128]{4,3,2,1,0:T(8,128)(2,1)S(1)}, bf16[2,16,3,128,128]{4,3,2,1,0:T(8,128)(2,1)}, u32[]{:S(2)}) copy-start(bf16[2,16,3,128,128]{4,3,2,1,0:T(8,128)(2,1)} %blocks_ref.3) | copy-start | bytes 9437188
  29.1 12.4 %collective-permute-start.2 = (bf16[256,1024]{1,0:T(8,128)(2,1)S(1)}, bf16[256,1024]{1,0:T(8,128)(2,1)S(1)}, u32[]{:S(2)}, u32[]{:S(2)}) collective-permute-start(bf16[256,1024]{1,0:T(8,128)(2,1)S(1)} %get-tuple-element.8), channel_id=1, source_target_pairs={{0,1},{1,0},{2,3},{3,2},{4,5},{5,4},{6,7},{7,6},{8,9},{9,8},{10,11... | collective-permute-start | bytes 1572872 | tf_op jit(solution)/shard_map/ppermute | solution.py:165
where the time goes:
time: 63.1 us; the launch traced here: 62.9 us
  blocking collectives  20.5 us (32%)
  Pallas kernels  16.6 us (26%)
  starting transfers between devices  16 us (25%)
  local copies, waits for them, and re-layouts  7.3 us (12%)
  waiting for transfers between devices  1.54 us (2%)
  other arithmetic  0.87 us (1%)
    all_to_all x1, blocking collectives, shards(): lax.all_to_all(chip_sum.reshape(chips, rows, params * width), AXIS, split...  20.5 us
    ppermute x1, starting transfers between devices, shards(): taken = lax.ppermute(give, AXIS, pairs(devices, 0))  10.9 us
    pallas_call x1, Pallas kernels, project(): pl.pallas_call(kernel, out_shape=(jax.ShapeDtypeStruct((half, params * wi...  6.24 us
    pallas_call x2, Pallas kernels, pick_blocks(): pl.pallas_call(kernel, out_shape=jax.ShapeDtypeStruct((halo,) + own.shape...  5.97 us
    unnamed x12, local copies, waits for them, and re-layouts  5.32 us
    pallas_call x1, Pallas kernels, own_terms(): pl.pallas_call(kernel, out_shape=terms, in_specs=[pl.BlockSpec(memory_spa...  4.34 us
    ppermute x1, starting transfers between devices, shards(): from_near = lax.ppermute(near, AXIS, pairs(devices, 0))  4.3 us
    transpose x1, local copies, waits for them, and re-layouts, shards(): turned = turned.transpose(1, 0, 2, 3).reshape(width, count * size)  1.98 us
  transfers between devices with their start and end apart: 3, of which 1 were waited for; matrix products, arithmetic and copies ran while one was open for 7% of the time, Pallas kernels for 12%

commit v1 on v0

--- a/solution.py
+++ b/solution.py
@@ -19,7 +19,8 @@
 def pick_blocks(own, sends, far):
     halo = sends.shape[1] // 2
 
-    def kernel(sends_ref, own_ref, out_ref, sems):
+    def kernel(sends_hbm, own_ref, out_ref, sends_ref, sems):
+        pltpu.sync_copy(sends_hbm, sends_ref)
         odd = lax.rem(lax.axis_index(AXIS), 2)
         first = (odd if far else 1 - odd) * halo
         copies = []
@@ -37,12 +38,15 @@
     return pl.pallas_call(
         kernel,
         out_shape=jax.ShapeDtypeStruct((halo,) + own.shape[1:], own.dtype),
-        in_specs=[pl.BlockSpec(memory_space=pltpu.SMEM), pl.BlockSpec(memory_space=pl.ANY)],
+        in_specs=[pl.BlockSpec(memory_space=pltpu.HBM)] * 2,
         out_specs=pl.BlockSpec(memory_space=pltpu.VMEM),
-        scratch_shapes=[pltpu.SemaphoreType.DMA((halo,))],
+        scratch_shapes=[pltpu.SMEM(sends.shape, sends.dtype), pltpu.SemaphoreType.DMA((halo,))],
         compiler_params=pltpu.CompilerParams(vmem_limit_bytes=VMEM_BYTES),
         cost_estimate=pl.CostEstimate(flops=0, bytes_accessed=2 * size, transcendentals=0),
-    )(sends, own)
+    )(
+        pltpu.with_memory_space_constraint(sends, pltpu.HBM),
+        pltpu.with_memory_space_constraint(own, pltpu.HBM),
+    )
 
 
 def own_terms(own, blocks, columns):
@@ -50,7 +54,7 @@
     width = own.shape[2]
 
     def kernel(columns_ref, own_ref, blocks_ref, out_ref):
-        @pl.loop(0, count, unroll=2)
+        @pl.loop(0, count, unroll=4)
         def _(row):
             at = pl.ds(pl.multiple_of(row * size, size), size)
             for param in range(params):
@@ -95,7 +99,7 @@
         list_ref[pl.ds(odd * halo, halo)] = far_ref[...]
         list_ref[pl.ds((1 - odd) * halo, halo)] = near_ref[...]
 
-        @pl.loop(0, count, unroll=2)
+        @pl.loop(0, count, unroll=4)
         def _(row):
             at = pl.ds(pl.multiple_of(row * size, size), size)
             for param in range(params):
@@ -112,17 +116,14 @@
                 )
                 image_ref[at, pl.ds(param * width, width)] = image.astype(image_ref.dtype)
 
-        mine = pl.ds(pl.multiple_of(odd * half, half), half)
-        other = pl.ds(pl.multiple_of((1 - odd) * half, half), half)
         step = 256 if width % 256 == 0 else width
         for at in range(0, params * width, step):
             cols = pl.ds(at, step)
-            give_ref[:, cols] = jnp.dot(
-                turned_ref[other], image_ref[:, cols], preferred_element_type=jnp.float32
-            ).astype(give_ref.dtype)
-            keep_ref[:, cols] = jnp.dot(
-                turned_ref[mine], image_ref[:, cols], preferred_element_type=jnp.float32
+            both = jnp.dot(
+                turned_ref[...], image_ref[:, cols], preferred_element_type=jnp.float32
             )
+            give_ref[:, cols] = both[:half].astype(give_ref.dtype)
+            keep_ref[:, cols] = both[half:]
 
     vmem = pl.BlockSpec(memory_space=pltpu.VMEM)
     flops = 2 * params * count * size * width * ((slots - 1) * size + 2 * half)
@@ -156,8 +157,9 @@
     from_far = lax.ppermute(far, AXIS, pairs(devices, 1))
     near = pick_blocks(own, sends, False)
     from_near = lax.ppermute(near, AXIS, pairs(devices, 0))
-    turned = basis.T.reshape(chips, 2, rows, count * size)
-    turned = turned.transpose(1, 0, 2, 3).reshape(width, count * size)
+    odd = lax.rem(lax.axis_index(AXIS), 2)
+    turned = basis.T.reshape(chips, 2, rows, count * size).transpose(1, 0, 2, 3)
+    turned = jnp.where(odd == 0, turned[::-1], turned).reshape(width, count * size)
 
     terms = own_terms(own, blocks, columns)
 

time: 63.1 us -> 60.3 us (0.956)
  other arithmetic: 0.87 us -> 3.87 us
  local copies, waits for them, and re-layouts: 7.3 us -> 4.4 us
  starting transfers between devices: 16 us -> 14.3 us
  Pallas kernels: 16.6 us -> 15.2 us
    select_n x0 -> x1, other arithmetic: none -> 3 us  [shards(): jnp.where(odd == 0, turned[::-1], turned).reshape(width, count * size)]
    transpose x1 -> x0, local copies, waits for them, and re-layouts: 1.98 us -> none  [shards(): turned = turned.transpose(1, 0, 2, 3).reshape(width, count * size)]
    ppermute x1, starting transfers between devices: 10.9 us -> 9.13 us  [shards(): taken = lax.ppermute(give, AXIS, pairs(devices, 0))]
    unnamed x12 -> x8, local copies, waits for them, and re-layouts: 5.32 us -> 4.26 us
    pallas_call x1, Pallas kernels: 6.24 us -> 5.53 us  [project(): pl.pallas_call(kernel, out_shape=(jax.ShapeDtypeStruct((half, params * wi...]
    pallas_call x1, Pallas kernels: 4.34 us -> 3.67 us  [own_terms(): pl.pallas_call(kernel, out_shape=terms, in_specs=[pl.BlockSpec(memory_spa...]
  transfers between devices with their start and end apart: 3 -> 3, of which waited for: 1 -> 1; matrix products, arithmetic and copies ran while one was open for 7% -> 9% of each run, Pallas kernels for 12% -> 11%
where the time goes in v1:
time: 60.3 us; the launch traced here: 60 us
  blocking collectives  20.5 us (34%)
  Pallas kernels  15.2 us (25%)
  starting transfers between devices  14.3 us (24%)
  local copies, waits for them, and re-layouts  4.4 us (7%)
  other arithmetic  3.87 us (6%)
  waiting for transfers between devices  1.54 us (3%)
    all_to_all x1, blocking collectives, shards(): lax.all_to_all(chip_sum.reshape(chips, rows, params * width), AXIS, split...  20.5 us
    ppermute x1, starting transfers between devices, shards(): taken = lax.ppermute(give, AXIS, pairs(devices, 0))  9.13 us
    pallas_call x2, Pallas kernels, pick_blocks(): pl.pallas_call(kernel, out_shape=jax.ShapeDtypeStruct((halo,) + own.shape...  6.03 us
    pallas_call x1, Pallas kernels, project(): pl.pallas_call(kernel, out_shape=(jax.ShapeDtypeStruct((half, params * wi...  5.53 us
    ppermute x1, starting transfers between devices, shards(): from_near = lax.ppermute(near, AXIS, pairs(devices, 0))  4.3 us
    unnamed x8, local copies, waits for them, and re-layouts  4.26 us
    pallas_call x1, Pallas kernels, own_terms(): pl.pallas_call(kernel, out_shape=terms, in_specs=[pl.BlockSpec(memory_spa...  3.67 us
    select_n x1, other arithmetic, shards(): jnp.where(odd == 0, turned[::-1], turned).reshape(width, count * size)  3 us
  transfers between devices with their start and end apart: 3, of which 1 were waited for; matrix products, arithmetic and copies ran while one was open for 9% of the time, Pallas kernels for 11%

profile of v1, /device:TPU:0, one launch (start us, length us, event | category | flops | bytes accessed | tf_op | source)
XLA Modules:
  0.0 60.0 jit_solution(13634989868009482992)
XLA Ops:
  0.0 3.0 %shard_map.47 = bf16[8,128,512]{2,1,0:T(8,128)(2,1)} custom-call(s32[1,16]{1,0:T(1,128)} %sends_hbm.3, bf16[16,128,512]{2,1,0:T(8,128)(2,1)} %bitcast.8), custom_call_target="tpu_custom_call" | custom-call | bytes 2097152 | tf_op jit(solution)/shard_map/pallas_call | solution.py:38
  3.0 0.0 copy-start
  3.0 0.9 %collective-permute-start = (bf16[8,128,512]{2,1,0:T(8,128)(2,1)}, bf16[8,128,512]{2,1,0:T(8,128)(2,1)S(1)}, u32[]{:S(2)}, u32[]{:S(2)}) collective-permute-start(bf16[8,128,512]{2,1,0:T(8,128)(2,1)} %shard_map.47), channel_id=1, source_target_pairs={{1,2},{2,1},{3,4},{4,3},{5,6},{6,5},{7,8},{8,7},{9,10},{10,9},{11,... | collective-permute-start | bytes 3145736 | tf_op jit(solution)/shard_map/ppermute | solution.py:157
  3.9 3.0 %shard_map.48 = bf16[8,128,512]{2,1,0:T(8,128)(2,1)} custom-call(s32[1,16]{1,0:T(1,128)} %sends_hbm.3, bf16[16,128,512]{2,1,0:T(8,128)(2,1)} %bitcast.9), custom_call_target="tpu_custom_call" | custom-call | bytes 2097152 | tf_op jit(solution)/shard_map/pallas_call | solution.py:38
  6.9 4.3 %collective-permute-start.1 = (bf16[8,128,512]{2,1,0:T(8,128)(2,1)}, bf16[8,128,512]{2,1,0:T(8,128)(2,1)}, u32[]{:S(2)}, u32[]{:S(2)}) collective-permute-start(bf16[8,128,512]{2,1,0:T(8,128)(2,1)} %shard_map.48), channel_id=1, source_target_pairs={{0,1},{1,0},{2,3},{3,2},{4,5},{5,4},{6,7},{7,6},{8,9},{9,8},{10,11... | collective-permute-start | bytes 3145736 | tf_op jit(solution)/shard_map/ppermute | solution.py:159
  11.2 0.0 copy-done
  11.2 0.0 copy-start.2
  11.2 2.4 %copy.8 = bf16[2048,512]{0,1:T(8,128)(2,1)} copy(bf16[2048,512]{1,0:T(8,128)(2,1)S(1)} %copy-done) | data formatting | bytes 4194304 | tf_op args[0]
  13.7 0.0 copy-done.2
  13.7 0.1 copy.11.columns_ref
  13.7 3.0 %reverse_select_fusion = bf16[2,8,32,2048]{3,2,0,1:T(8,128)(2,1)S(1)} fusion(bf16[2,8,32,2048]{3,2,0,1:T(8,128)(2,1)} %bitcast.12, pred[]{:T(512)S(6)} %eq.3), kind=kLoop, calls=%fused_computation | loop fusion | flops 1048576 | bytes 4194305 | tf_op jit(solution)/shard_map/jit(_where)/select_n | solution.py:162
  16.8 0.0 copy-start.1
  16.8 0.1 copy.9
  16.9 1.7 %copy-done.1 = bf16[2,16,3,128,128]{4,3,2,1,0:T(8,128)(2,1)S(1)} copy-done((bf16[2,16,3,128,128]{4,3,2,1,0:T(8,128)(2,1)S(1)}, bf16[2,16,3,128,128]{4,3,2,1,0:T(8,128)(2,1)}, u32[]{:S(2)}) %copy-start.1) | copy-done | bytes 3145752
  18.6 3.7 %shard_map.46.terms_ref = f32[2,2048,512]{2,1,0:T(8,128)S(1)} custom-call(s32[2,16,2]{2,1,0:T(8,128)S(1)} %copy.11.columns_ref, bf16[16,128,512]{2,1,0:T(8,128)(2,1)S(1)} %bitcast.10, bf16[2,16,3,128,128]{4,3,2,1,0:T(8,128)(2,1)S(1)} %copy-done.1), custom_call_target="tpu_custom_call" | custom-call | flops 1610612736 | bytes 13631488 | tf_op jit(solution)/shard_map/pallas_call | solution.py:75
  22.3 0.0 collective-permute-done.far_ref
  22.3 0.0 collective-permute-done.1.near_ref
  22.3 5.5 %shard_map.49 = (f32[256,1024]{1,0:T(8,128)S(1)}, bf16[256,1024]{1,0:T(8,128)(2,1)S(1)}) custom-call(s32[2,16,2]{2,1,0:T(8,128)S(1)} %copy.11.columns_ref, bf16[512,2048]{1,0:T(8,128)(2,1)S(1)} %bitcast.11, f32[2,2048,512]{2,1,0:T(8,128)S(1)} %shard_map.46.terms_ref, bf16[8,128,512]{2,1,0:T(8,128)(2,1)S(1)} %collective-permute-done.far_ref, ...), custom_call_target="tpu_custom_call" | custom-call | flops 3221225472 | bytes 15728640 | tf_op jit(solution)/shard_map/pallas_call | solution.py:131
  27.9 9.1 %collective-permute-start.2 = (bf16[256,1024]{1,0:T(8,128)(2,1)S(1)}, bf16[256,1024]{1,0:T(8,128)(2,1)S(1)}, u32[]{:S(2)}, u32[]{:S(2)}) collective-permute-start(bf16[256,1024]{1,0:T(8,128)(2,1)S(1)} %get-tuple-element.8), channel_id=1, source_target_pairs={{0,1},{1,0},{2,3},{3,2},{4,5},{5,4},{6,7},{7,6},{8,9},{9,8},{10,11... | collective-permute-start | bytes 1572872 | tf_op jit(solution)/shard_map/ppermute | solution.py:167
  37.0 1.5 %collective-permute-done.2 = bf16[256,1024]{1,0:T(8,128)(2,1)S(1)} collective-permute-done((bf16[256,1024]{1,0:T(8,128)(2,1)S(1)}, bf16[256,1024]{1,0:T(8,128)(2,1)S(1)}, u32[]{:S(2)}, u32[]{:S(2)}) %collective-permute-start.2) | collective-permute-done | bytes 524320 | tf_op jit(solution)/shard_map/ppermute | solution.py:167
  38.6 0.1 add_convert_fusion
  38.7 20.5 %all_to_all.5 = bf16[8,32,1024]{2,1,0:T(8,128)(2,1)S(1)} all-to-all(bf16[8,32,1024]{2,1,0:T(8,128)(2,1)S(1)} %bitcast.13), channel_id=1, replica_groups={{0,2,4,6,8,10,12,14},{1,3,5,7,9,11,13,15},{16,18,20,22,24,26,28,30},{17..., dimensions={0} | all-to-all | bytes 1048576 | tf_op jit(solution)/shard_map/all_to_all | solution.py:170
  59.2 0.7 %convert_reduce_fusion = f32[32,1024]{1,0:T(8,128)} fusion(bf16[8,32,1024]{2,1,0:T(8,128)(2,1)S(1)} %all_to_all.5), kind=kLoop, calls=%fused_computation.1 | loop fusion | flops 491520 | bytes 655360 | tf_op jit(solution)/shard_map/reduce_sum | solution.py:174
Async XLA Ops:
  3.0 8.2 %copy-start = (bf16[2048,512]{1,0:T(8,128)(2,1)S(1)}, bf16[2048,512]{1,0:T(8,128)(2,1)}, u32[]{:S(2)}) copy-start(bf16[2048,512]{1,0:T(8,128)(2,1)} %param.4) | copy-start | bytes 6291460
  3.0 19.3 %collective-permute-start = (bf16[8,128,512]{2,1,0:T(8,128)(2,1)}, bf16[8,128,512]{2,1,0:T(8,128)(2,1)S(1)}, u32[]{:S(2)}, u32[]{:S(2)}) collective-permute-start(bf16[8,128,512]{2,1,0:T(8,128)(2,1)} %shard_map.47), channel_id=1, source_target_pairs={{1,2},{2,1},{3,4},{4,3},{5,6},{6,5},{7,8},{8,7},{9,10},{10,9},{11,... | collective-permute-start | bytes 3145736 | tf_op jit(solution)/shard_map/ppermute | solution.py:157
  6.9 15.4 %collective-permute-start.1 = (bf16[8,128,512]{2,1,0:T(8,128)(2,1)}, bf16[8,128,512]{2,1,0:T(8,128)(2,1)}, u32[]{:S(2)}, u32[]{:S(2)}) collective-permute-start(bf16[8,128,512]{2,1,0:T(8,128)(2,1)} %shard_map.48), channel_id=1, source_target_pairs={{0,1},{1,0},{2,3},{3,2},{4,5},{5,4},{6,7},{7,6},{8,9},{9,8},{10,11... | collective-permute-start | bytes 3145736 | tf_op jit(solution)/shard_map/ppermute | solution.py:159
  11.2 2.4 %copy-start.2 = (s32[2,16,2]{1,2,0:T(2,128)S(1)}, s32[2,16,2]{1,2,0:T(2,128)}, u32[]{:S(2)}) copy-start(s32[2,16,2]{1,2,0:T(2,128)} %param.6) | copy-start | bytes 772
  16.8 1.9 %copy-start.1 = (bf16[2,16,3,128,128]{4,3,2,1,0:T(8,128)(2,1)S(1)}, bf16[2,16,3,128,128]{4,3,2,1,0:T(8,128)(2,1)}, u32[]{:S(2)}) copy-start(bf16[2,16,3,128,128]{4,3,2,1,0:T(8,128)(2,1)} %blocks_ref.3) | copy-start | bytes 9437188
  27.9 10.7 %collective-permute-start.2 = (bf16[256,1024]{1,0:T(8,128)(2,1)S(1)}, bf16[256,1024]{1,0:T(8,128)(2,1)S(1)}, u32[]{:S(2)}, u32[]{:S(2)}) collective-permute-start(bf16[256,1024]{1,0:T(8,128)(2,1)S(1)} %get-tuple-element.8), channel_id=1, source_target_pairs={{0,1},{1,0},{2,3},{3,2},{4,5},{5,4},{6,7},{7,6},{8,9},{9,8},{10,11... | collective-permute-start | bytes 1572872 | tf_op jit(solution)/shard_map/ppermute | solution.py:167

commit v2 on v1

v2 whole, which is shorter than its diff:
```python
import jax
import jax.numpy as jnp
from jax import lax
from jax.experimental import pallas as pl
from jax.experimental.pallas import tpu as pltpu
from jax.sharding import PartitionSpec as P

AXIS = "mesh"
LANES = 128
VMEM_BYTES = 28 * 1024 * 1024
VMEM = pl.BlockSpec(memory_space=pltpu.VMEM)
SMEM = pl.BlockSpec(memory_space=pltpu.SMEM)
PARAMETERS = pltpu.CompilerParams(vmem_limit_bytes=VMEM_BYTES)


def cost(flops, moved):
    return pl.CostEstimate(flops=flops, bytes_accessed=moved, transcendentals=0)


def pairs(count, first):
    both = []
    for low in range(first, count - 1, 2):
        both += [(low, low + 1), (low + 1, low)]
    return both


def chunks(width):
    first = width // 4
    if first % LANES:
        return [(0, width)]
    return [(0, first), (first, width - first)]


def copy_listed(own_ref, sends_ref, part, far_ref, near_ref):
    halo = far_ref.shape[0]
    odd = lax.rem(lax.axis_index(AXIS), 2)
    for place in range(halo):
        far_ref[place] = own_ref[sends_ref[0, odd * halo + place], :, pl.ds(*part)]
    for place in range(halo):
        near_ref[place] = own_ref[sends_ref[0, (1 - odd) * halo + place], :, pl.ds(*part)]


def pick_first(own, sends, part):
    count, size, _ = own.shape
    listed = jax.ShapeDtypeStruct((sends.shape[1] // 2, size, part[1]), own.dtype)

    def kernel(sends_hbm, own_hbm, own_ref, far_ref, near_ref, sends_ref, sems):
        lists = pltpu.make_async_copy(sends_hbm, sends_ref, sems.at[0])
        load = pltpu.make_async_copy(own_hbm, own_ref, sems.at[1])
        lists.start()
        load.start()
        lists.wait()
        load.wait()
        copy_listed(own_ref, sends_ref, part, far_ref, near_ref)

    return pl.pallas_call(
        kernel,
        out_shape=(jax.ShapeDtypeStruct(own.shape, own.dtype), listed, listed),
        in_specs=[pl.BlockSpec(memory_space=pltpu.HBM)] * 2,
        out_specs=(VMEM,) * 3,
        scratch_shapes=[pltpu.SMEM(sends.shape, sends.dtype), pltpu.SemaphoreType.DMA((2,))],
        compiler_params=PARAMETERS,
        cost_estimate=cost(0, 4 * own.size),
    )(
        pltpu.with_memory_space_constraint(sends, pltpu.HBM),
        pltpu.with_memory_space_constraint(own, pltpu.HBM),
    )


def pick_next(own, sends, part):
    listed = jax.ShapeDtypeStruct((sends.shape[1] // 2, own.shape[1], part[1]), own.dtype)

    def kernel(sends_hbm, own_ref, far_ref, near_ref, sends_ref):
        pltpu.sync_copy(sends_hbm, sends_ref)
        copy_listed(own_ref, sends_ref, part, far_ref, near_ref)

    return pl.pallas_call(
        kernel,
        out_shape=(listed, listed),
        in_specs=[pl.BlockSpec(memory_space=pltpu.HBM), VMEM],
        out_specs=(VMEM,) * 2,
        scratch_shapes=[pltpu.SMEM(sends.shape, sends.dtype)],
        compiler_params=PARAMETERS,
        cost_estimate=cost(0, 0),
    )(pltpu.with_memory_space_constraint(sends, pltpu.HBM), own)


def own_terms(own, blocks, columns, start, span):
    params, count, slots, size, _ = blocks.shape

    def kernel(columns_ref, own_ref, blocks_ref, out_ref):
        cols = pl.ds(start, span)

        @pl.loop(0, count, unroll=4)
        def _(row):
            at = pl.ds(pl.multiple_of(row * size, size), size)
            for param in range(params):
                left, right = [blocks_ref[param, row, 0]], [own_ref[row, :, cols]]
                for slot in range(1, slots):
                    block = blocks_ref[param, row, slot]
                    column = columns_ref[param, row, slot - 1]
                    left.append(jnp.where(column < count, block, jnp.zeros_like(block)))
                    right.append(own_ref[jnp.minimum(column, count - 1), :, cols])
                out_ref[param, at] = jnp.dot(
                    jnp.concatenate(left, axis=1),
                    jnp.concatenate(right, axis=0),
                    preferred_element_type=jnp.float32,
                )

    terms = jax.ShapeDtypeStruct((params, count * size, span), jnp.float32)
    return pl.pallas_call(
        kernel,
        out_shape=terms,
        in_specs=[SMEM, VMEM, VMEM],
        out_specs=VMEM,
        compiler_params=PARAMETERS,
        cost_estimate=cost(0, 0),
    )(columns, own, blocks)


def transposed(own, devices):
    count, size, width = own.shape
    chips, rows = devices // 2, width // devices
    if rows % 16:
        turned = own.reshape(count * size, width).T.reshape(chips, 2, rows, count * size)
        return turned.transpose(1, 0, 2, 3).reshape(width, count * size)

    def kernel(own_ref, out_ref):
        @pl.loop(0, count)
        def _(block):
            cols = pl.ds(pl.multiple_of(block * size, size), size)
            turned = own_ref[block].T
            for device in range(devices):
                chip, core = divmod(device, 2)
                out_ref[pl.ds((core * chips + chip) * rows, rows), cols] = (
                    turned[device * rows : (device + 1) * rows]
                )

    return pl.pallas_call(
        kernel,
        out_shape=jax.ShapeDtypeStruct((width, count * size), own.dtype),
        in_specs=[VMEM],
        out_specs=VMEM,
        compiler_params=PARAMETERS,
        cost_estimate=cost(0, 0),
    )(own)


def image_and_give(turned, terms, far, near, blocks, columns):
    params, count, slots, size, _ = blocks.shape
    halo, _, span = far.shape
    half = turned.shape[0] // 2

    def kernel(
        columns_ref, turned_ref, terms_ref, far_ref, near_ref, blocks_ref,
        image_ref, give_ref, list_ref,
    ):
        odd = lax.rem(lax.axis_index(AXIS), 2)
        list_ref[pl.ds(odd * halo, halo)] = far_ref[...]
        list_ref[pl.ds((1 - odd) * halo, halo)] = near_ref[...]

        @pl.loop(0, count, unroll=4)
        def _(row):
            at = pl.ds(pl.multiple_of(row * size, size), size)
            for param in range(params):
                left, right = [], []
                for slot in range(1, slots):
                    block = blocks_ref[param, row, slot]
                    column = columns_ref[param, row, slot - 1]
                    left.append(jnp.where(column < count, jnp.zeros_like(block), block))
                    right.append(list_ref[jnp.maximum(column - count, 0)])
                image = terms_ref[param, at] + jnp.dot(
                    jnp.concatenate(left, axis=1),
                    jnp.concatenate(right, axis=0),
                    preferred_element_type=jnp.float32,
                )
                image_ref[at, pl.ds(param * span, span)] = image.astype(image_ref.dtype)

        other = pl.ds(pl.multiple_of((1 - odd) * half, half), half)
        for cols in steps(params * span):
            give_ref[:, cols] = jnp.dot(
                turned_ref[other], image_ref[:, cols], preferred_element_type=jnp.float32
            ).astype(give_ref.dtype)

    rows = count * size
    flops = 2 * params * rows * span * ((slots - 1) * size + half)
    moved = 4 * terms.size + 2 * (half * rows + 2 * far.size + blocks.size + params * span * (rows + half))
    return pl.pallas_call(
        kernel,
        out_shape=(
            jax.ShapeDtypeStruct((rows, params * span), jnp.bfloat16),
            jax.ShapeDtypeStruct((half, params * span), jnp.bfloat16),
        ),
        in_specs=[SMEM] + [VMEM] * 5,
        out_specs=(VMEM,) * 2,
        scratch_shapes=[pltpu.VMEM((2 * halo, size, span), far.dtype)],
        compiler_params=PARAMETERS,
        cost_estimate=cost(flops, moved),
    )(columns, turned, terms, far, near, blocks)


def steps(columns):
    step = 2 * LANES if columns % (2 * LANES) == 0 else columns
    return [pl.ds(at, step) for at in range(0, columns, step)]


def keep_rows(turned, image):
    half, rows = turned.shape[0] // 2, turned.shape[1]
    columns = image.shape[1]

    def kernel(turned_ref, image_ref, keep_ref):
        odd = lax.rem(lax.axis_index(AXIS), 2)
        mine = pl.ds(pl.multiple_of(odd * half, half), half)
        for cols in steps(columns):
            keep_ref[:, cols] = jnp.dot(
                turned_ref[mine], image_ref[:, cols], preferred_element_type=jnp.float32
            )

    return pl.pallas_call(
        kernel,
        out_shape=jax.ShapeDtypeStruct((half, columns), jnp.float32),
        in_specs=[VMEM] * 2,
        out_specs=VMEM,
        compiler_params=PARAMETERS,
        cost_estimate=cost(
            2 * half * rows * columns, 2 * rows * (half + columns) + 4 * half * columns
        ),
    )(turned, image)


def add_chips(received, params, width):
    rows = received[0].shape[1]
    ranges = chunks(width)

    def kernel(*refs):
        out_ref = refs[-1]
        for (start, span), ref in zip(ranges, refs):
            total = jnp.sum(ref[...].astype(jnp.float32), axis=0)
            for param in range(params):
                out_ref[:, pl.ds(param * width + start, span)] = total[:, param * span : (param + 1) * span]

    return pl.pallas_call(
        kernel,
        out_shape=jax.ShapeDtypeStruct((rows, params * width), jnp.float32),
        in_specs=[VMEM] * len(received),
        out_specs=VMEM,
        compiler_params=PARAMETERS,
        cost_estimate=cost(0, sum(2 * part.size for part in received)),
    )(*received)


def shards(basis, blocks, columns, sends):
    params, count, _, size, _ = blocks.shape
    width = basis.shape[1]
    devices = lax.axis_size(AXIS)
    chips = devices // 2
    rows = width // devices
    ranges = chunks(width)
    near_pairs = pairs(devices, 0)

    own, far, near = pick_first(basis.reshape(count, size, width), sends, ranges[0])
    listed = [(far, near)]
    terms = [own_terms(own, blocks, columns, *ranges[0])]
    own, terms[0] = lax.optimization_barrier((own, terms[0]))
    listed += [pick_next(own, sends, part) for part in ranges[1:]]
    halos = [
        (lax.ppermute(far, AXIS, pairs(devices, 1)), lax.ppermute(near, AXIS, near_pairs))
        for far, near in listed
    ]
    terms += [own_terms(own, blocks, columns, *part) for part in ranges[1:]]
    turned = transposed(own, devices)
    groups = [list(range(core, devices, 2)) for core in range(2)]
    received = []
    for (_, span), (far, near), term in zip(ranges, halos, terms):
        if received:
            received[-1], term = lax.optimization_barrier((received[-1], term))
        image, give = image_and_give(turned, term, far, near, blocks, columns)
        taken = lax.ppermute(give, AXIS, near_pairs)
        keep = keep_rows(turned, image)
        chip_sum = (keep + taken.astype(jnp.float32)).astype(jnp.bfloat16)
        parts = lax.all_to_all(
            chip_sum.reshape(chips, rows, params * span), AXIS,
            split_axis=0, concat_axis=0, axis_index_groups=groups, tiled=True,
        )
        received.append(parts)
    return add_chips(received, params, width)


def solution(mesh):
    placed = (
        P(("grp", "mesh"), None),
        P(None, ("grp", "mesh"), None, None, None),
        P(None, ("grp", "mesh"), None),
        P(("grp", "mesh"), None),
    )
    return jax.shard_map(
        shards, mesh=mesh, in_specs=placed, out_specs=P(("grp", "mesh"), None), check_vma=False
    )
```

time: 60.3 us -> 69.7 us (1.16)
  local copies, waits for them, and re-layouts: 4.4 us -> 14.4 us
  Pallas kernels: 15.2 us -> 20.4 us
  other arithmetic: 3.87 us -> 0.75 us
  blocking collectives: 20.5 us -> 18.1 us
    unnamed x8 -> x21, local copies, waits for them, and re-layouts: 4.26 us -> 14.4 us
    ppermute x3 -> x6, starting transfers between devices: 14.3 us -> 8.96 us  [the longest x2 7.27 us: shards(): lax.ppermute(near, AXIS, near_pairs)]
    pallas_call x4 -> x10, Pallas kernels: 15.2 us -> 20.4 us  [the longest x2 6.47 us: image_and_give(): pl.pallas_call(kernel, out_shape=(jax.ShapeDtypeStruct((rows, params * sp...]
    all_to_all x0 -> x1, starting transfers between devices: none -> 4.8 us  [shards(): lax.all_to_all(chip_sum.reshape(chips, rows, params * span), AXIS, split_...]
    select_n x1 -> x0, other arithmetic: 3 us -> none  [shards(): jnp.where(odd == 0, turned[::-1], turned).reshape(width, count * size)]
    all_to_all x1, blocking collectives: 20.5 us -> 18.1 us  [shards(): lax.all_to_all(chip_sum.reshape(chips, rows, params * span), AXIS, split_...]
    reduce_sum x1 -> x0, other arithmetic: 0.73 us -> none  [shards(): return jnp.sum(parts.astype(jnp.float32), axis=0)]
    ppermute x3 -> x6, waiting for transfers between devices: 1.54 us -> 1.48 us  [the longest x2 1.46 us: shards(): taken = lax.ppermute(give, AXIS, near_pairs)]
  transfers between devices with their start and end apart: 3 -> 7, of which waited for: 1 -> 2; matrix products, arithmetic and copies ran while one was open for 9% -> 1% of each run, Pallas kernels for 11% -> 19%
where the time goes in v2:
time: 69.7 us; the launch traced here: 69.1 us
  Pallas kernels  20.4 us (29%)
  blocking collectives  18.1 us (26%)
  local copies, waits for them, and re-layouts  14.4 us (21%)
  starting transfers between devices  13.8 us (20%)
  waiting for transfers between devices  1.48 us (2%)
  other arithmetic  0.75 us (1%)
    all_to_all x1, blocking collectives, shards(): lax.all_to_all(chip_sum.reshape(chips, rows, params * span), AXIS, split_...  18.1 us
    unnamed x21, local copies, waits for them, and re-layouts  14.4 us
    ppermute x2, starting transfers between devices, shards(): lax.ppermute(near, AXIS, near_pairs)  7.27 us
    pallas_call x2, Pallas kernels, image_and_give(): pl.pallas_call(kernel, out_shape=(jax.ShapeDtypeStruct((rows, params * sp...  6.47 us
    pallas_call x2, Pallas kernels, own_terms(): pl.pallas_call(kernel, out_shape=terms, in_specs=[SMEM, VMEM, VMEM], out_...  5.8 us
    all_to_all x1, starting transfers between devices, shards(): lax.all_to_all(chip_sum.reshape(chips, rows, params * span), AXIS, split_...  4.8 us
    pallas_call x1, Pallas kernels, pick_first(): pl.pallas_call(kernel, out_shape=(jax.ShapeDtypeStruct(own.shape, own.dty...  2.5 us
    pallas_call x1, Pallas kernels, pick_next(): pl.pallas_call(kernel, out_shape=(listed, listed), in_specs=[pl.BlockSpec...  2.06 us
  transfers between devices with their start and end apart: 7, of which 2 were waited for; matrix products, arithmetic and copies ran while one was open for 1% of the time, Pallas kernels for 19%

profile of v2, /device:TPU:0, one launch (start us, length us, event | category | flops | bytes accessed | tf_op | source)
XLA Modules:
  0.0 69.1 jit_solution(7048112985311637619)
XLA Ops:
  0.0 0.0 copy-start.9
  0.0 2.5 %shard_map.46 = (bf16[16,128,512]{2,1,0:T(8,128)(2,1)S(1)}, bf16[8,128,128]{2,1,0:T(8,128)(2,1)}, bf16[8,128,128]{2,1,0:T(8,128)(2,1)}) custom-call(s32[1,16]{1,0:T(1,128)} %sends_hbm.3, bf16[16,128,512]{2,1,0:T(8,128)(2,1)} %bitcast.3), custom_call_target="tpu_custom_call" | custom-call | bytes 4194304 | tf_op jit(solution)/shard_map/pallas_call | solution.py:56
  2.5 0.0 copy-start.4
  2.5 0.7 collective-permute-start
  3.2 4.3 %collective-permute-start.1 = (bf16[8,128,128]{2,1,0:T(8,128)(2,1)}, bf16[8,128,128]{2,1,0:T(8,128)(2,1)S(1)}, u32[]{:S(2)}, u32[]{:S(2)}) collective-permute-start(bf16[8,128,128]{2,1,0:T(8,128)(2,1)} %get-tuple-element.22), channel_id=1, source_target_pairs={{0,1},{1,0},{2,3},{3,2},{4,5},{5,4},{6,7},{7,6},{8,9},{9,8},{10,11... | collective-permute-start | bytes 786440 | tf_op jit(solution)/shard_map/ppermute | solution.py:267
  7.6 0.0 copy-done.9
  7.6 0.1 copy.5.columns_ref
  7.7 0.0 copy-start
  7.7 1.9 %copy-done = bf16[2,16,3,128,128]{4,3,2,1,0:T(8,128)(2,1)S(1)} copy-done((bf16[2,16,3,128,128]{4,3,2,1,0:T(8,128)(2,1)S(1)}, bf16[2,16,3,128,128]{4,3,2,1,0:T(8,128)(2,1)}, u32[]{:S(2)}) %copy-start) | copy-done | bytes 3145752
  9.5 2.3 %shard_map.47.terms_ref = f32[2,2048,128]{2,1,0:T(8,128)S(1)} custom-call(s32[2,16,2]{2,1,0:T(8,128)S(1)} %copy.5.columns_ref, bf16[16,128,512]{2,1,0:T(8,128)(2,1)S(1)} %get-tuple-element.19.own_ref, bf16[2,16,3,128,128]{4,3,2,1,0:T(8,128)(2,1)S(1)} %copy-done), custom_call_target="tpu_custom_call" | custom-call | tf_op jit(solution)/shard_map/pallas_call | solution.py:111
  11.8 0.0 copy-done.4
  11.8 2.1 %shard_map.52 = (bf16[8,128,384]{2,1,0:T(8,128)(2,1)}, bf16[8,128,384]{2,1,0:T(8,128)(2,1)}) custom-call(s32[1,16]{1,0:T(1,128)} %sends_hbm.3, bf16[16,128,512]{2,1,0:T(8,128)(2,1)S(1)} %get-tuple-element.19.own_ref), custom_call_target="tpu_custom_call" | custom-call | tf_op jit(solution)/shard_map/pallas_call | solution.py:77
  13.9 0.7 %collective-permute-start.3 = (bf16[8,128,384]{2,1,0:T(8,128)(2,1)}, bf16[8,128,384]{2,1,0:T(8,128)(2,1)S(1)}, u32[]{:S(2)}, u32[]{:S(2)}) collective-permute-start(bf16[8,128,384]{2,1,0:T(8,128)(2,1)} %get-tuple-element.27), channel_id=1, source_target_pairs={{1,2},{2,1},{3,4},{4,3},{5,6},{6,5},{7,8},{8,7},{9,10},{10,9},{11,... | collective-permute-start | bytes 2359304 | tf_op jit(solution)/shard_map/ppermute | solution.py:267
  14.6 0.0 copy-start.1
  14.6 2.9 %collective-permute-start.4 = (bf16[8,128,384]{2,1,0:T(8,128)(2,1)}, bf16[8,128,384]{2,1,0:T(8,128)(2,1)}, u32[]{:S(2)}, u32[]{:S(2)}) collective-permute-start(bf16[8,128,384]{2,1,0:T(8,128)(2,1)} %get-tuple-element.28), channel_id=1, source_target_pairs={{0,1},{1,0},{2,3},{3,2},{4,5},{5,4},{6,7},{7,6},{8,9},{9,8},{10,11... | collective-permute-start | bytes 2359304 | tf_op jit(solution)/shard_map/ppermute | solution.py:267
  17.5 0.0 copy-start.5
  17.5 1.6 %copy-done.5 = bf16[16,128,512]{2,1,0:T(8,128)(2,1)S(1)} copy-done((bf16[16,128,512]{2,1,0:T(8,128)(2,1)S(1)}, bf16[16,128,512]{2,1,0:T(8,128)(2,1)}, u32[]{:S(2)}) %copy-start.5) | copy-done | bytes 2097176
  19.1 1.5 %shard_map.48.turned_ref = bf16[512,2048]{1,0:T(8,128)(2,1)S(1)} custom-call(bf16[16,128,512]{2,1,0:T(8,128)(2,1)S(1)} %copy-done.5), custom_call_target="tpu_custom_call" | custom-call | tf_op jit(solution)/shard_map/pallas_call | solution.py:139
  20.6 0.0 collective-permute-done.far_ref
  20.6 0.0 collective-permute-done.1.near_ref
  20.6 0.0 copy-done.1
  20.7 2.5 %shard_map.49 = (bf16[2048,256]{1,0:T(8,128)(2,1)S(1)}, bf16[256,256]{1,0:T(8,128)(2,1)S(1)}) custom-call(s32[2,16,2]{2,1,0:T(8,128)S(1)} %copy.5.columns_ref, bf16[512,2048]{1,0:T(8,128)(2,1)S(1)} %shard_map.48.turned_ref, f32[2,2048,128]{2,1,0:T(8,128)S(1)} %shard_map.47.terms_ref, bf16[8,128,128]{2,1,0:T(8,128)(2,1)S(1)} %collective-permute-done.far_ref, ...), custom_call_target="tpu_custom_call" | custom-call | flops 536870912 | bytes 7995392 | tf_op jit(solution)/shard_map/pallas_call | solution.py:188
  23.1 0.2 collective-permute-start.2
  23.4 0.4 shard_map.50
  23.8 0.7 %collective-permute-done.2 = bf16[256,256]{1,0:T(8,128)(2,1)S(1)} collective-permute-done((bf16[256,256]{1,0:T(8,128)(2,1)S(1)}, bf16[256,256]{1,0:T(8,128)(2,1)S(1)}, u32[]{:S(2)}, u32[]{:S(2)}) %collective-permute-start.2) | collective-permute-done | bytes 131104 | tf_op jit(solution)/shard_map/ppermute | solution.py:278
  24.6 0.7 add_convert_fusion.1
  25.2 4.8 %all-to-all-start = ((bf16[8,32,256]{2,1,0:T(8,128)(2,1)}), bf16[8,32,256]{2,1,0:T(8,128)(2,1)S(1)}, u32[]{:S(2)}, u32[]{:S(2)}) async-start(bf16[8,32,256]{2,1,0:T(8,128)(2,1)} %bitcast.1), calls=%async_computation | async-start | bytes 262144 | tf_op jit(solution)/shard_map/all_to_all | solution.py:281
  30.0 0.0 copy-start.2
  30.0 1.9 %copy-done.2 = bf16[2,16,3,128,128]{4,3,2,1,0:T(8,128)(2,1)S(1)} copy-done((bf16[2,16,3,128,128]{4,3,2,1,0:T(8,128)(2,1)S(1)}, bf16[2,16,3,128,128]{4,3,2,1,0:T(8,128)(2,1)}, u32[]{:S(2)}) %copy-start.2) | copy-done | bytes 3145752
  31.9 0.0 copy-start.6
  31.9 1.6 %copy-done.6 = bf16[16,128,512]{2,1,0:T(8,128)(2,1)S(1)} copy-done((bf16[16,128,512]{2,1,0:T(8,128)(2,1)S(1)}, bf16[16,128,512]{2,1,0:T(8,128)(2,1)}, u32[]{:S(2)}) %copy-start.6) | copy-done | bytes 2097176
  33.5 3.5 %shard_map.51.terms_ref = f32[2,2048,384]{2,1,0:T(8,128)S(1)} custom-call(s32[2,16,2]{2,1,0:T(8,128)S(1)} %copy.5.columns_ref, bf16[16,128,512]{2,1,0:T(8,128)(2,1)S(1)} %copy-done.6, bf16[2,16,3,128,128]{4,3,2,1,0:T(8,128)(2,1)S(1)} %copy-done.2), custom_call_target="tpu_custom_call" | custom-call | tf_op jit(solution)/shard_map/pallas_call | solution.py:111
  37.0 0.0 copy-start.7
  37.0 2.7 %copy-done.7 = f32[2,2048,384]{2,1,0:T(8,128)} copy-done((f32[2,2048,384]{2,1,0:T(8,128)}, f32[2,2048,384]{2,1,0:T(8,128)S(1)}, u32[]{:S(2)}) %copy-start.7) | copy-done | bytes 6291480
  39.7 0.0 all-to-all-done.refs_0_
  39.7 0.0 collective-permute-done.3.far_ref
  39.7 0.0 collective-permute-done.4.near_ref
  39.7 0.0 copy-start.3
  39.7 1.9 %copy-done.3 = bf16[2,16,3,128,128]{4,3,2,1,0:T(8,128)(2,1)S(1)} copy-done((bf16[2,16,3,128,128]{4,3,2,1,0:T(8,128)(2,1)S(1)}, bf16[2,16,3,128,128]{4,3,2,1,0:T(8,128)(2,1)}, u32[]{:S(2)}) %copy-start.3) | copy-done | bytes 3145752
  41.6 0.0 copy-start.8
  41.6 2.8 %copy-done.8 = f32[2,2048,384]{2,1,0:T(8,128)S(1)} copy-done((f32[2,2048,384]{2,1,0:T(8,128)S(1)}, f32[2,2048,384]{2,1,0:T(8,128)}, u32[]{:S(2)}) %copy-start.8) | copy-done | bytes 6291480
  44.4 4.0 %shard_map.53 = (bf16[2048,768]{1,0:T(8,128)(2,1)S(1)}, bf16[256,768]{1,0:T(8,128)(2,1)S(1)}) custom-call(s32[2,16,2]{2,1,0:T(8,128)S(1)} %copy.5.columns_ref, bf16[512,2048]{1,0:T(8,128)(2,1)S(1)} %shard_map.48.turned_ref, f32[2,2048,384]{2,1,0:T(8,128)S(1)} %copy-done.8, bf16[8,128,384]{2,1,0:T(8,128)(2,1)S(1)} %collective-permute-done.3.far_ref, ...), custom_call_target="tpu_custom_call" | custom-call | flops 1610612736 | bytes 15597568 | tf_op jit(solution)/shard_map/pallas_call | solution.py:188
  48.4 0.1 collective-permute-start.5
  48.5 1.0 %shard_map.54 = f32[256,768]{1,0:T(8,128)S(1)} custom-call(bf16[512,2048]{1,0:T(8,128)(2,1)S(1)} %shard_map.48.turned_ref, bf16[2048,768]{1,0:T(8,128)(2,1)S(1)} %get-tuple-element.29.image_ref), custom_call_target="tpu_custom_call" | custom-call | flops 805306368 | bytes 4980736 | tf_op jit(solution)/shard_map/pallas_call | solution.py:219
  49.5 0.7 %collective-permute-done.5 = bf16[256,768]{1,0:T(8,128)(2,1)S(1)} collective-permute-done((bf16[256,768]{1,0:T(8,128)(2,1)S(1)}, bf16[256,768]{1,0:T(8,128)(2,1)S(1)}, u32[]{:S(2)}, u32[]{:S(2)}) %collective-permute-start.5) | collective-permute-done | bytes 393248 | tf_op jit(solution)/shard_map/ppermute | solution.py:278
  50.2 0.1 add_convert_fusion
  50.3 18.1 %all_to_all.10.refs_1_ = bf16[8,32,768]{2,1,0:T(8,128)(2,1)S(1)} all-to-all(bf16[8,32,768]{2,1,0:T(8,128)(2,1)S(1)} %bitcast.4), channel_id=1, replica_groups={{0,2,4,6,8,10,12,14},{1,3,5,7,9,11,13,15},{16,18,20,22,24,26,28,30},{17..., dimensions={0} | all-to-all | bytes 786432 | tf_op jit(solution)/shard_map/all_to_all | solution.py:281
  68.4 0.7 %shard_map.55 = f32[32,1024]{1,0:T(8,128)} custom-call(bf16[8,32,256]{2,1,0:T(8,128)(2,1)S(1)} %all-to-all-done.refs_0_, bf16[8,32,768]{2,1,0:T(8,128)(2,1)S(1)} %all_to_all.10.refs_1_), custom_call_target="tpu_custom_call" | custom-call | bytes 524288 | tf_op jit(solution)/shard_map/pallas_call | solution.py:242
Async XLA Ops:
  0.0 7.6 %copy-start.9 = (s32[2,16,2]{1,2,0:T(2,128)S(1)}, s32[2,16,2]{1,2,0:T(2,128)}, u32[]{:S(2)}) copy-start(s32[2,16,2]{1,2,0:T(2,128)} %param.6) | copy-start | bytes 772
  2.5 9.3 %copy-start.4 = (bf16[16,128,512]{2,1,0:T(8,128)(2,1)}, bf16[16,128,512]{2,1,0:T(8,128)(2,1)S(1)}, u32[]{:S(2)}) copy-start(bf16[16,128,512]{2,1,0:T(8,128)(2,1)S(1)} %get-tuple-element.19.own_ref) | copy-start | bytes 6291460
  2.5 18.1 %collective-permute-start = (bf16[8,128,128]{2,1,0:T(8,128)(2,1)}, bf16[8,128,128]{2,1,0:T(8,128)(2,1)S(1)}, u32[]{:S(2)}, u32[]{:S(2)}) collective-permute-start(bf16[8,128,128]{2,1,0:T(8,128)(2,1)} %get-tuple-element.21), channel_id=1, source_target_pairs={{1,2},{2,1},{3,4},{4,3},{5,6},{6,5},{7,8},{8,7},{9,10},{10,9},{11,... | collective-permute-start | bytes 786440 | tf_op jit(solution)/shard_map/ppermute | solution.py:267
  3.2 17.4 %collective-permute-start.1 = (bf16[8,128,128]{2,1,0:T(8,128)(2,1)}, bf16[8,128,128]{2,1,0:T(8,128)(2,1)S(1)}, u32[]{:S(2)}, u32[]{:S(2)}) collective-permute-start(bf16[8,128,128]{2,1,0:T(8,128)(2,1)} %get-tuple-element.22), channel_id=1, source_target_pairs={{0,1},{1,0},{2,3},{3,2},{4,5},{5,4},{6,7},{7,6},{8,9},{9,8},{10,11... | collective-permute-start | bytes 786440 | tf_op jit(solution)/shard_map/ppermute | solution.py:267
  7.7 1.9 %copy-start = (bf16[2,16,3,128,128]{4,3,2,1,0:T(8,128)(2,1)S(1)}, bf16[2,16,3,128,128]{4,3,2,1,0:T(8,128)(2,1)}, u32[]{:S(2)}) copy-start(bf16[2,16,3,128,128]{4,3,2,1,0:T(8,128)(2,1)} %blocks_ref.7) | copy-start | bytes 9437188
  13.9 25.8 %collective-permute-start.3 = (bf16[8,128,384]{2,1,0:T(8,128)(2,1)}, bf16[8,128,384]{2,1,0:T(8,128)(2,1)S(1)}, u32[]{:S(2)}, u32[]{:S(2)}) collective-permute-start(bf16[8,128,384]{2,1,0:T(8,128)(2,1)} %get-tuple-element.27), channel_id=1, source_target_pairs={{1,2},{2,1},{3,4},{4,3},{5,6},{6,5},{7,8},{8,7},{9,10},{10,9},{11,... | collective-permute-start | bytes 2359304 | tf_op jit(solution)/shard_map/ppermute | solution.py:267
  14.6 6.0 %copy-start.1 = (bf16[2,16,3,128,128]{4,3,2,1,0:T(8,128)(2,1)S(1)}, bf16[2,16,3,128,128]{4,3,2,1,0:T(8,128)(2,1)}, u32[]{:S(2)}) copy-start(bf16[2,16,3,128,128]{4,3,2,1,0:T(8,128)(2,1)} %blocks_ref.7) | copy-start | bytes 9437188
  14.6 25.1 %collective-permute-start.4 = (bf16[8,128,384]{2,1,0:T(8,128)(2,1)}, bf16[8,128,384]{2,1,0:T(8,128)(2,1)}, u32[]{:S(2)}, u32[]{:S(2)}) collective-permute-start(bf16[8,128,384]{2,1,0:T(8,128)(2,1)} %get-tuple-element.28), channel_id=1, source_target_pairs={{0,1},{1,0},{2,3},{3,2},{4,5},{5,4},{6,7},{7,6},{8,9},{9,8},{10,11... | collective-permute-start | bytes 2359304 | tf_op jit(solution)/shard_map/ppermute | solution.py:267
  17.5 1.6 %copy-start.5 = (bf16[16,128,512]{2,1,0:T(8,128)(2,1)S(1)}, bf16[16,128,512]{2,1,0:T(8,128)(2,1)}, u32[]{:S(2)}) copy-start(bf16[16,128,512]{2,1,0:T(8,128)(2,1)} %copy-done.4) | copy-start | bytes 6291460
  23.1 1.4 %collective-permute-start.2 = (bf16[256,256]{1,0:T(8,128)(2,1)S(1)}, bf16[256,256]{1,0:T(8,128)(2,1)S(1)}, u32[]{:S(2)}, u32[]{:S(2)}) collective-permute-start(bf16[256,256]{1,0:T(8,128)(2,1)S(1)} %get-tuple-element.24), channel_id=1, source_target_pairs={{0,1},{1,0},{2,3},{3,2},{4,5},{5,4},{6,7},{7,6},{8,9},{9,8},{10,11... | collective-permute-start | bytes 393224 | tf_op jit(solution)/shard_map/ppermute | solution.py:278
  25.2 14.5 %all-to-all-start = ((bf16[8,32,256]{2,1,0:T(8,128)(2,1)}), bf16[8,32,256]{2,1,0:T(8,128)(2,1)S(1)}, u32[]{:S(2)}, u32[]{:S(2)}) async-start(bf16[8,32,256]{2,1,0:T(8,128)(2,1)} %bitcast.1), calls=%async_computation | async-start | bytes 262144 | tf_op jit(solution)/shard_map/all_to_all | solution.py:281
  30.0 1.9 %copy-start.2 = (bf16[2,16,3,128,128]{4,3,2,1,0:T(8,128)(2,1)S(1)}, bf16[2,16,3,128,128]{4,3,2,1,0:T(8,128)(2,1)}, u32[]{:S(2)}) copy-start(bf16[2,16,3,128,128]{4,3,2,1,0:T(8,128)(2,1)} %blocks_ref.7) | copy-start | bytes 9437188
  31.9 1.6 %copy-start.6 = (bf16[16,128,512]{2,1,0:T(8,128)(2,1)S(1)}, bf16[16,128,512]{2,1,0:T(8,128)(2,1)}, u32[]{:S(2)}) copy-start(bf16[16,128,512]{2,1,0:T(8,128)(2,1)} %copy-done.4) | copy-start | bytes 6291460
  37.0 2.7 %copy-start.7 = (f32[2,2048,384]{2,1,0:T(8,128)}, f32[2,2048,384]{2,1,0:T(8,128)S(1)}, u32[]{:S(2)}) copy-start(f32[2,2048,384]{2,1,0:T(8,128)S(1)} %shard_map.51.terms_ref) | copy-start | bytes 18874372
  39.7 1.9 %copy-start.3 = (bf16[2,16,3,128,128]{4,3,2,1,0:T(8,128)(2,1)S(1)}, bf16[2,16,3,128,128]{4,3,2,1,0:T(8,128)(2,1)}, u32[]{:S(2)}) copy-start(bf16[2,16,3,128,128]{4,3,2,1,0:T(8,128)(2,1)} %blocks_ref.7) | copy-start | bytes 9437188
  41.6 2.8 %copy-start.8 = (f32[2,2048,384]{2,1,0:T(8,128)S(1)}, f32[2,2048,384]{2,1,0:T(8,128)}, u32[]{:S(2)}) copy-start(f32[2,2048,384]{2,1,0:T(8,128)} %copy-done.7) | copy-start | bytes 18874372
  48.4 1.8 %collective-permute-start.5 = (bf16[256,768]{1,0:T(8,128)(2,1)S(1)}, bf16[256,768]{1,0:T(8,128)(2,1)S(1)}, u32[]{:S(2)}, u32[]{:S(2)}) collective-permute-start(bf16[256,768]{1,0:T(8,128)(2,1)S(1)} %get-tuple-element.30), channel_id=1, source_target_pairs={{0,1},{1,0},{2,3},{3,2},{4,5},{5,4},{6,7},{7,6},{8,9},{9,8},{10,11... | collective-permute-start | bytes 1179656 | tf_op jit(solution)/shard_map/ppermute | solution.py:278
